TPU v7x, 128 devices: a whole 4x4x4 slice. The times are simulated.
128 devices in a mesh: dp: 8 (over x, core), seq: 16 (over z, y).
Axes of the slice: x: 4, y: 4, z: 4, core: 2. Of those that a mesh axis runs over, the one named last changes fastest.
Arguments:
- trunk: bfloat16 [8, 4096, 1536], P('dp', 'seq'), may hold values from -34 to 34
- skip: bfloat16 [8, 8192, 1536], P('dp', 'seq'), may hold values from -6 to 6
- valid_bins: int32 [8], P('dp'), may hold values from 2048 to 4096, as said below
- query_weight: bfloat16 [1536, 256], replicated
- key_weight: bfloat16 [1536, 256], replicated
- value_weight: bfloat16 [1536, 768], replicated, may hold values from -0.15625 to 0.15625
- out_weight: bfloat16 [768, 1536], replicated, may hold values from -0.21875 to 0.21875
- depth_weight: float32 [3, 1536], replicated, may hold values from -3 to 3
- point_weight: bfloat16 [1536, 1536], replicated, may hold values from -0.15625 to 0.15625
- cotangent: bfloat16 [8, 8192, 1536], P('dp', 'seq'), may hold values from -6 to 6
Outputs:
- grad_pointwise: bfloat16 [1536, 1536], replicated
- grad_depthwise: float32 [3, 1536], replicated
- grad_skip: bfloat16 [8, 8192, 1536], P('dp', 'seq')
Inputs may be any that keep to these rules, and one draw needn't show every extreme that they name: Bins at or past a window's valid_bins are padding; in every draw some window is whole.
All inputs are finite; a program needn't handle non-finite values.
Results may differ from a plain program's by a relative error of at most 0.017.
Values may be sent and summed in bfloat16 or wider, within the bound.
No kernel may reach another device: no remote copies, remote signals or barrier semaphores. Data moves between devices by JAX's collectives and lax.ppermute only.
A program may use at most 128 MiB of HBM per device.

v0:
```python
from functools import partial
import math
import jax
import jax.numpy as jnp
from jax import lax
from jax.sharding import PartitionSpec as P

H = 4
DH = 64
DV = 192


def padded_2(cells, sides, width):
    for axis, dim in sides:
        count = lax.axis_size(axis)
        ends = count - 1
        head = lax.slice_in_dim(cells, 0, width, axis=dim)
        tail = lax.slice_in_dim(cells, cells.shape[dim] - width, cells.shape[dim], axis=dim)
        cells = jnp.concatenate(
            [
                lax.ppermute(tail, axis, [(i, (i + 1) % count) for i in range(ends)]),
                cells,
                lax.ppermute(head, axis, [((i + 1) % count, i) for i in range(ends)]),
            ],
            axis=dim,
        )
    return cells


def local(
    trunk,
    skip,
    valid_bins,
    query_weight,
    key_weight,
    value_weight,
    out_weight,
    depth_weight,
    point_weight,
    cotangent,
):
    tokens = trunk[0]
    row_count = tokens.shape[0]
    score_scale = 1.0 / math.sqrt(DH)
    queries = (
        jnp.dot(tokens, query_weight, preferred_element_type=jnp.float32)
        .astype(jnp.bfloat16)
        .reshape(row_count, H, DH)
    )
    keys = jnp.dot(tokens, key_weight, preferred_element_type=jnp.float32).astype(jnp.bfloat16)
    values = jnp.dot(tokens, value_weight, preferred_element_type=jnp.float32).astype(jnp.bfloat16)
    limit = valid_bins[0]
    running_max = jnp.full((H, row_count), -1e30, jnp.float32)
    weighted = jnp.zeros((row_count, H, DV), jnp.float32)
    key_piece = lax.all_gather(keys, "seq", axis=0, tiled=True)
    value_piece = lax.all_gather(values, "seq", axis=0, tiled=True)
    width = key_piece.shape[0]
    key_heads = key_piece.reshape(width, H, DH)
    value_heads = value_piece.reshape(width, H, DV)
    scores = (
        jnp.einsum("qhd,khd->hqk", queries, key_heads, preferred_element_type=jnp.float32)
        * score_scale
    )
    places = jnp.arange(width, dtype=jnp.int32)
    scores = jnp.where(places[None, None, :] < limit, scores, -1e30)
    fresh_max = jnp.maximum(running_max, jnp.max(scores, axis=2))
    shrink = jnp.exp(running_max - fresh_max)
    weights_raw = jnp.exp(scores - fresh_max[:, :, None])
    running_total = jnp.sum(weights_raw, axis=2)
    update = jnp.einsum(
        "hqk,khd->qhd",
        weights_raw.astype(jnp.bfloat16),
        value_heads,
        preferred_element_type=jnp.float32,
    )
    weighted = weighted * shrink.T[:, :, None] + update
    running_max, running_total, weighted = (fresh_max, running_total, weighted)
    mixed = (weighted / running_total.T[:, :, None]).reshape(row_count, H * DV)
    attended = (mixed * lax.rsqrt(jnp.mean(mixed * mixed, axis=1, keepdims=True) + 1e-05)).astype(
        jnp.bfloat16
    )
    hidden = (
        tokens.astype(jnp.float32)
        + jnp.dot(attended, out_weight, preferred_element_type=jnp.float32)
    ).astype(jnp.bfloat16)
    upsampled = (
        jnp.repeat(hidden, 2, axis=0).astype(jnp.float32) + skip[0].astype(jnp.float32)
    ).astype(jnp.bfloat16)
    padded = padded_2(upsampled, (("seq", 0),), 1)
    pre_act = (
        depth_weight[0] * padded[:-2]
        + depth_weight[1] * padded[1:-1]
        + depth_weight[2] * padded[2:]
    )
    act_value, pullback = jax.vjp(partial(jax.nn.gelu, approximate=True), pre_act)
    activated = act_value.astype(jnp.bfloat16)
    upstream = cotangent[0]
    grad_act = lax.dot_general(
        upstream, point_weight, (((1,), (1,)), ((), ())), preferred_element_type=jnp.float32
    )
    grad_pre = pullback(grad_act)[0].astype(jnp.bfloat16)
    fine_rows = grad_pre.shape[0]
    grad_wide = grad_pre.astype(jnp.float32)
    depth_term = jnp.stack(
        [
            jnp.sum(padded[offset : offset + fine_rows].astype(jnp.float32) * grad_wide, axis=0)
            for offset in range(3)
        ]
    )
    grad_padded = padded_2(grad_pre, (("seq", 0),), 1)
    grad_skip = (
        depth_weight[0] * grad_padded[2:]
        + depth_weight[1] * grad_padded[1:-1]
        + depth_weight[2] * grad_padded[:-2]
    ).astype(jnp.bfloat16)
    norm_scale = 1.0 / math.sqrt(lax.axis_size("dp") * lax.axis_size("seq") * fine_rows)
    point_term = lax.dot_general(
        activated, upstream, (((0,), (0,)), ((), ())), preferred_element_type=jnp.float32
    )
    point_total, depth_total = lax.psum((point_term, depth_term), ("dp", "seq"))
    grad_pointwise = (point_total * norm_scale).astype(jnp.bfloat16)
    return (grad_pointwise, depth_total * norm_scale, grad_skip[None])


def solution(mesh):
    return jax.shard_map(
        local,
        mesh=mesh,
        in_specs=(
            P("dp", "seq", None),
            P("dp", "seq", None),
            P("dp"),
            P(),
            P(),
            P(),
            P(),
            P(),
            P(),
            P("dp", "seq", None),
        ),
        out_specs=(P(), P(), P("dp", "seq", None)),
        check_vma=False,
    )
```

profile of v0, /device:TPU:1, one launch (start us, length us, event | category | flops | bytes accessed | tf_op | source)
XLA Modules:
  0.0 349.5 jit_solution(12524377417579679030)
XLA Ops:
  7.2 2.6 convolution_convert_fusion.1
  9.9 3.4 convolution_convert_fusion
  14.1 1.6 convolution_convert_fusion.2
  15.7 42.6 %all-gather.3.cloned.1.call-done = bf16[4096,256]{1,0:T(8,128)(2,1)} async-done(((bf16[256,256]{1,0:T(8,128)(2,1)}), bf16[4096,256]{1,0:T(8,128)(2,1)}) %all-gather.3.cloned.1.call-update) | async-done | bytes 2097168 | tf_op jit(solution)/shard_map/all_gather | solution.py:55
  58.2 4.1 %copy.15 = bf16[4096,256]{0,1:T(8,128)(2,1)} copy(bf16[4096,256]{1,0:T(8,128)(2,1)} %all-gather.3.cloned.1.call-done) | data formatting | bytes 4194304 | tf_op jit(solution)/shard_map/all_gather | solution.py:55
  62.3 4.1 %fusion = (f32[4,256]{1,0:T(4,128)S(1)}, f32[4,256,4096]{2,1,0:T(8,128)S(1)}) fusion(pred[4096]{0:T(1024)(128)(4,1)S(1)} %iota_compare_fusion, bf16[256,4,64]{0,2,1:T(8,128)(2,1)S(1)} %bitcast.49, bf16[4096,4,64]{0,2,1:T(8,128)(2,1)} %bitcast.47), kind=kOutput, calls=%fused_computation.2 | convolution fusion | flops 549452800 | bytes 19013632 | tf_op jit(solution)/shard_map/qhd,khd->hqk/dot_general | solution.py:61
  66.4 5.9 %copy-done.2 = f32[4,256,4096]{2,1,0:T(8,128)} copy-done((f32[4,256,4096]{2,1,0:T(8,128)}, f32[4,256,4096]{2,1,0:T(8,128)S(1)}, u32[]{:S(2)}) %copy-start.2) | copy-done | bytes 16777240
  72.4 4.0 %fusion.1 = f32[4,256]{1,0:T(4,128)S(1)} fusion(f32[4,256,4096]{2,1,0:T(8,128)S(1)} %get-tuple-element.17, f32[4,256]{1,0:T(4,128)S(1)} %get-tuple-element.15, pred[4096]{0:T(1024)(128)(4,1)S(1)} %iota_compare_fusion), kind=kLoop, calls=%fused_computation.3 | loop fusion | flops 16776192 | bytes 16789504 | tf_op jit(solution)/shard_map/reduce_sum | solution.py:69
  76.4 46.3 %all-gather.5.cloned.1.call-done = bf16[4096,768]{1,0:T(8,128)(2,1)} async-done(((bf16[256,768]{1,0:T(8,128)(2,1)}), bf16[4096,768]{1,0:T(8,128)(2,1)}) %all-gather.5.cloned.1.call-update) | async-done | bytes 6291472 | tf_op jit(solution)/shard_map/all_gather | solution.py:56
  122.7 8.6 %copy.16 = bf16[4096,768]{0,1:T(8,128)(2,1)} copy(bf16[4096,768]{1,0:T(8,128)(2,1)} %all-gather.5.cloned.1.call-done) | data formatting | bytes 12582912 | tf_op jit(solution)/shard_map/all_gather | solution.py:56
  131.3 10.3 %multiply_reduce_fusion = (f32[256]{0:T(256)S(1)}, f32[256,4,192]{0,2,1:T(8,128)S(1)}) fusion(f32[256,4]{0,1:T(4,128)S(1)} %bitcast.50, bf16[4096,4,192]{0,2,1:T(8,128)(2,1)} %bitcast.48, f32[4,256,4096]{2,1,0:T(8,128)} %copy-done.2, f32[4,256]{1,0:T(4,128)S(1)} %get-tuple-element.15, pred[4096]{0:T(1024)(128)(4,1)S(1)} %iota_compare_fusion, ...), kind=kOutput, calls=%fused_computation.68 | convolution fusion | flops 1628176128 | bytes 23872512 | tf_op jit(solution)/shard_map/hqk,khd->qhd/dot_general | solution.py:70
  142.5 2.7 broadcast_in_dim.33
  145.2 5.2 %convert_element_type.79 = f32[512,1536]{1,0:T(8,128)} reshape(f32[256,2,1536]{2,1,0:T(2,128)} %broadcast_in_dim.33) | data formatting | bytes 6291456 | tf_op jit(solution)/shard_map/convert_element_type | solution.py:87
  150.5 2.9 fusion.24
  153.4 3.1 collective-permute-start
  156.6 1.5 collective-permute-start.1
  158.1 2.8 collective-permute-done.1
  160.9 6.6 %fusion.27 = f32[1536,1536]{1,0:T(8,128)} fusion(bf16[512,1536]{1,0:T(8,128)(2,1)S(1)} %fusion.24, bf16[1,1536]{1,0:T(2,128)(2,1)S(1)} %collective-permute-done.1, bf16[1,1536]{1,0:T(2,128)(2,1)S(1)} %collective-permute-done, bf16[1,512,1536]{2,1,0:T(8,128)(2,1)S(1)} %copy-done.5, f32[1536]{0:T(1024)S(1)} %get-tuple-element.7, ...), kind=kOutput, calls=%fused_computation.41 | convolution fusion | flops 2434007040 | bytes 12607488 | tf_op jit(solution)/shard_map/dot_general | solution.py:117
  167.5 7.5 %fusion.17 = bf16[512,1536]{1,0:T(8,128)(2,1)S(1)} fusion(bf16[1,1536]{1,0:T(2,128)(2,1)S(1)} %collective-permute-done.1, bf16[512,1536]{1,0:T(8,128)(2,1)S(1)} %fusion.24, bf16[1,1536]{1,0:T(2,128)(2,1)S(1)} %collective-permute-done, bf16[1536,1536]{1,0:T(8,128)(2,1)} %param.18, bf16[1,512,1536]{2,1,0:T(8,128)(2,1)} %param.19, ...), kind=kOutput, calls=%fused_computation.28 | convolution fusion | flops 2442657792 | bytes 9461760 | tf_op jit(solution)/shard_map/dot_general | solution.py:98
  176.4 4.0 %collective-permute-start.3 = (bf16[1,1536]{1,0:T(2,128)(2,1)S(1)}, bf16[1,1536]{1,0:T(2,128)(2,1)S(1)}, u32[]{:S(2)}, u32[]{:S(2)}) collective-permute-start(bf16[1,1536]{1,0:T(2,128)(2,1)S(1)} %get-tuple-element.11), channel_id=1, source_target_pairs={{0,1},{1,2},{2,3},{3,4},{4,5},{5,6},{6,7},{7,8},{8,9},{9,10},{10,1... | collective-permute-start | bytes 9224 | tf_op jit(solution)/shard_map/ppermute | solution.py:21
  181.1 3.5 %fusion.18 = (f32[1536]{0:T(1024)S(1)}, f32[1536]{0:T(1024)S(1)}, f32[1536]{0:T(1024)S(1)}, bf16[1,512,1536]{2,1,0:T(8,128)(2,1)}) fusion(bf16[512,1536]{1,0:T(8,128)(2,1)S(1)} %fusion.17, bf16[512,1536]{1,0:T(8,128)(2,1)S(1)} %fusion.24, bf16[1,1536]{1,0:T(2,128)(2,1)S(1)} %collective-permute-done, bf16[1,1536]{1,0:T(2,128)(2,1)S(1)} %collective-permute-done.1, ...), kind=kLoop, calls=%fused_computation.29 | loop fusion | flops 23588352 | bytes 4767744 | tf_op jit(solution)/shard_map/reduce_sum | solution.py:106
  184.7 74.9 %psum.15 = f32[3,1536]{1,0:T(4,128)S(1)} all-reduce(f32[3,1536]{1,0:T(4,128)S(1)} %pad_maximum_fusion.5), channel_id=1, replica_groups=mesh['dp'=8,'seq'=16] {'dp','seq'}, use_global_device_ids=true, to_apply=%region_7.8 | all-reduce | flops 4608 | bytes 36864 | tf_op jit(solution)/shard_map/psum | solution.py:120
  260.2 75.5 %all-reduce.2.cloned.1.call-done = f32[1536,1536]{1,0:T(8,128)} async-done(((f32[1536,1536]{1,0:T(8,128)}), f32[1536,1536]{1,0:T(8,128)}) %all-reduce.2.cloned.1.call-update) | async-done | bytes 9437200 | tf_op jit(solution)/shard_map/psum | solution.py:120
  335.7 7.2 %multiply_convert_fusion = bf16[1536,1536]{1,0:T(8,128)(2,1)} fusion(f32[1536,1536]{1,0:T(8,128)} %all-reduce.2.cloned.1.call-done), kind=kLoop, calls=%fused_computation.5 | loop fusion | flops 4718592 | bytes 14155776 | tf_op jit(solution)/shard_map/convert_element_type | solution.py:121
  (34 shorter events, 3.9 us)
Async XLA Ops:
  7.2 134.5 %copy-start = (bf16[768,1536]{1,0:T(8,128)(2,1)S(1)}, bf16[768,1536]{1,0:T(8,128)(2,1)}, u32[]{:S(2)}) copy-start(bf16[768,1536]{1,0:T(8,128)(2,1)} %param.16) | copy-start | bytes 7077892
  7.2 6.9 %copy-start.3 = (bf16[1,256,1536]{2,1,0:T(8,128)(2,1)S(1)}, bf16[1,256,1536]{2,1,0:T(8,128)(2,1)}, u32[]{:S(2)}) copy-start(bf16[1,256,1536]{2,1,0:T(8,128)(2,1)} %param.10) | copy-start | bytes 2359300
  7.2 51.0 %all-gather.3.cloned.1.call-start = ((), (), s32[]{:S(2)}) async-start(), calls=%async_computation | async-start | bytes 2228224 | tf_op jit(solution)/shard_map/all_gather | solution.py:55
  9.8 112.8 %all-gather.5.cloned.1.call-start = ((), (), s32[]{:S(2)}) async-start(), calls=%async_computation.1 | async-start | bytes 6684672 | tf_op jit(solution)/shard_map/all_gather | solution.py:56
  13.4 322.4 %all-reduce.2.cloned.1.call-start = ((), (), s32[]{:S(2)}) async-start(), calls=%async_computation.2 | async-start | bytes 18874368 | tf_op jit(solution)/shard_map/psum | solution.py:120
  66.4 6.0 %copy-start.2 = (f32[4,256,4096]{2,1,0:T(8,128)}, f32[4,256,4096]{2,1,0:T(8,128)S(1)}, u32[]{:S(2)}) copy-start(f32[4,256,4096]{2,1,0:T(8,128)S(1)} %get-tuple-element.17) | copy-start | bytes 50331652
  150.5 7.6 %copy-start.4 = (f32[3,1536]{1,0:T(4,128)S(1)}, f32[3,1536]{1,0:T(4,128)}, u32[]{:S(2)}) copy-start(f32[3,1536]{1,0:T(4,128)} %param.17) | copy-start | bytes 55300
  150.5 10.4 %copy-start.5 = (bf16[1,512,1536]{2,1,0:T(8,128)(2,1)S(1)}, bf16[1,512,1536]{2,1,0:T(8,128)(2,1)}, u32[]{:S(2)}) copy-start(bf16[1,512,1536]{2,1,0:T(8,128)(2,1)} %param.19) | copy-start | bytes 4718596
  153.4 4.7 %collective-permute-start = (bf16[1,1536]{1,0:T(2,128)(2,1)S(1)}, bf16[1,1536]{1,0:T(2,128)(2,1)S(1)}, u32[]{:S(2)}, u32[]{:S(2)}) collective-permute-start(bf16[1,1536]{1,0:T(2,128)(2,1)S(1)} %get-tuple-element.12), channel_id=1, source_target_pairs={{0,1},{1,2},{2,3},{3,4},{4,5},{5,6},{6,7},{7,8},{8,9},{9,10},{10,1... | collective-permute-start | bytes 9224 | tf_op jit(solution)/shard_map/ppermute | solution.py:21
  156.6 4.4 %collective-permute-start.1 = (bf16[1,1536]{1,0:T(2,128)(2,1)S(1)}, bf16[1,1536]{1,0:T(2,128)(2,1)S(1)}, u32[]{:S(2)}, u32[]{:S(2)}) collective-permute-start(bf16[1,1536]{1,0:T(2,128)(2,1)S(1)} %get-tuple-element.13), channel_id=1, source_target_pairs={{1,0},{2,1},{3,2},{4,3},{5,4},{6,5},{7,6},{8,7},{9,8},{10,9},{11,1... | collective-permute-start | bytes 9224 | tf_op jit(solution)/shard_map/ppermute | solution.py:23
  175.1 5.3 %collective-permute-start.2 = (bf16[1,1536]{1,0:T(2,128)(2,1)S(1)}, bf16[1,1536]{1,0:T(2,128)(2,1)S(1)}, u32[]{:S(2)}, u32[]{:S(2)}) collective-permute-start(bf16[1,1536]{1,0:T(2,128)(2,1)S(1)} %get-tuple-element.10), channel_id=1, source_target_pairs={{1,0},{2,1},{3,2},{4,3},{5,4},{6,5},{7,6},{8,7},{9,8},{10,9},{11,1... | collective-permute-start | bytes 9224 | tf_op jit(solution)/shard_map/ppermute | solution.py:23
  176.4 4.8 %collective-permute-start.3 = (bf16[1,1536]{1,0:T(2,128)(2,1)S(1)}, bf16[1,1536]{1,0:T(2,128)(2,1)S(1)}, u32[]{:S(2)}, u32[]{:S(2)}) collective-permute-start(bf16[1,1536]{1,0:T(2,128)(2,1)S(1)} %get-tuple-element.11), channel_id=1, source_target_pairs={{0,1},{1,2},{2,3},{3,4},{4,5},{5,6},{6,7},{7,8},{8,9},{9,10},{10,1... | collective-permute-start | bytes 9224 | tf_op jit(solution)/shard_map/ppermute | solution.py:21
  335.7 7.2 %copy-start.1 = (bf16[768,1536]{1,0:T(8,128)(2,1)S(1)}, bf16[768,1536]{1,0:T(8,128)(2,1)}, u32[]{:S(2)}) copy-start(bf16[768,1536]{1,0:T(8,128)(2,1)} %param.16) | copy-start | bytes 7077892
Sparse Core Ops, SparseCore 0:
  10.7 47.4 all-gather.2
  60.9 61.6 all-gather.4
  167.6 168.0 all-reduce.1
where the time goes:
time: 350 us
  waiting for transfers between devices  168 us (48%)
  blocking collectives  74.9 us (21%)
  matrix products  36.9 us (11%)
  local copies, waits for them, and re-layouts  26.7 us (8%)
  other arithmetic  18.4 us (5%)
  between operations  14.6 us (4%)
  starting transfers between devices  9.98 us (3%)
    psum x1, waiting for transfers between devices, local(): point_total, depth_total = lax.psum((point_term, depth_term), ('dp', 'seq'))  75.5 us
    psum x1, blocking collectives, local(): point_total, depth_total = lax.psum((point_term, depth_term), ('dp', 'seq'))  74.9 us
    all_gather x1, waiting for transfers between devices, local(): value_piece = lax.all_gather(values, 'seq', axis=0, tiled=True)  46.3 us
    all_gather x1, waiting for transfers between devices, local(): key_piece = lax.all_gather(keys, 'seq', axis=0, tiled=True)  42.6 us
    dot_general x1, matrix products, local(): jnp.einsum('hqk,khd->qhd', weights_raw.astype(jnp.bfloat16), value_heads,...  10.3 us
    all_gather x1, local copies, waits for them, and re-layouts, local(): value_piece = lax.all_gather(values, 'seq', axis=0, tiled=True)  8.63 us
    dot_general x1, matrix products, local(): lax.dot_general(upstream, point_weight, (((1,), (1,)), ((), ())), preferr...  7.54 us
    convert_element_type x1, other arithmetic, local(): grad_pointwise = (point_total * norm_scale).astype(jnp.bfloat16)  7.24 us
  transfers between devices with their start and end apart: 7, of which 5 were waited for; matrix products, arithmetic and copies ran while one was open for 8% of the time, Pallas kernels for 0%

commit v1 on v0

--- a/solution.py
+++ b/solution.py
@@ -52,8 +52,11 @@
     limit = valid_bins[0]
     running_max = jnp.full((H, row_count), -1e30, jnp.float32)
     weighted = jnp.zeros((row_count, H, DV), jnp.float32)
-    key_piece = lax.all_gather(keys, "seq", axis=0, tiled=True)
-    value_piece = lax.all_gather(values, "seq", axis=0, tiled=True)
+    key_piece, value_piece = jnp.split(
+        lax.all_gather(jnp.concatenate([keys, values], axis=1), "seq", axis=0, tiled=True),
+        [keys.shape[1]],
+        axis=1,
+    )
     width = key_piece.shape[0]
     key_heads = key_piece.reshape(width, H, DH)
     value_heads = value_piece.reshape(width, H, DV)

time: 350 us -> 338 us (0.966)
  waiting for transfers between devices: 168 us -> 151 us
  local copies, waits for them, and re-layouts: 26.7 us -> 31.7 us
    split x0 -> x4, local copies, waits for them, and re-layouts: none -> 21.8 us  [local(): jnp.split(lax.all_gather(jnp.concatenate([keys, values], axis=1), 'seq',...]
    all_gather x2 -> x1, waiting for transfers between devices: 88.9 us -> 72 us  [local(): lax.all_gather(jnp.concatenate([keys, values], axis=1), 'seq', axis=0, ti...]
    all_gather x2 -> x0, local copies, waits for them, and re-layouts: 12.7 us -> none  [the longest x1 8.63 us: local(): value_piece = lax.all_gather(values, 'seq', axis=0, tiled=True)]
    unnamed x12, local copies, waits for them, and re-layouts: 5.96 us -> 1.69 us
  transfers between devices with their start and end apart: 7 -> 6, of which waited for: 5 -> 4; matrix products, arithmetic and copies ran while one was open for 8% -> 4% of each run, Pallas kernels for 0% -> 0%
where the time goes in v1:
time: 338 us; the launch traced here: 337 us
  waiting for transfers between devices  151 us (45%)
  blocking collectives  74.9 us (22%)
  matrix products  35.5 us (11%)
  local copies, waits for them, and re-layouts  31.7 us (9%)
  other arithmetic  19.3 us (6%)
  between operations  14.9 us (4%)
  starting transfers between devices  9.94 us (3%)
    psum x1, waiting for transfers between devices, local(): point_total, depth_total = lax.psum((point_term, depth_term), ('dp', 'seq'))  75.5 us
    psum x1, blocking collectives, local(): point_total, depth_total = lax.psum((point_term, depth_term), ('dp', 'seq'))  74.9 us
    all_gather x1, waiting for transfers between devices, local(): lax.all_gather(jnp.concatenate([keys, values], axis=1), 'seq', axis=0, ti...  72 us
    split x4, local copies, waits for them, and re-layouts, local(): jnp.split(lax.all_gather(jnp.concatenate([keys, values], axis=1), 'seq',...  21.8 us
    dot_general x1, matrix products, local(): jnp.einsum('hqk,khd->qhd', weights_raw.astype(jnp.bfloat16), value_heads,...  10.3 us
    dot_general x1, matrix products, local(): lax.dot_general(upstream, point_weight, (((1,), (1,)), ((), ())), preferr...  7.54 us
    convert_element_type x1, other arithmetic, local(): grad_pointwise = (point_total * norm_scale).astype(jnp.bfloat16)  7.24 us
    ppermute x2, starting transfers between devices, padded_2(): lax.ppermute(tail, axis, [(i, (i + 1) % count) for i in range(ends)])  7.1 us
  transfers between devices with their start and end apart: 6, of which 4 were waited for; matrix products, arithmetic and copies ran while one was open for 4% of the time, Pallas kernels for 0%

profile of v1, /device:TPU:1, one launch (start us, length us, event | category | flops | bytes accessed | tf_op | source)
XLA Modules:
  0.0 337.3 jit_solution(5054450176500487343)
XLA Ops:
  7.2 1.9 convolution_convert_fusion.1
  9.3 2.7 convolution_convert_fusion
  13.6 1.6 convolution_convert_fusion.2
  15.2 72.0 %all-gather.2.cloned.1.call-done = bf16[4096,1024]{1,0:T(8,128)(2,1)} async-done(((bf16[256,1024]{1,0:T(8,128)(2,1)}), bf16[4096,1024]{1,0:T(8,128)(2,1)}) %all-gather.2.cloned.1.call-update) | async-done | bytes 8388624 | tf_op jit(solution)/shard_map/all_gather | solution.py:56
  87.2 5.9 %split.9 = bf16[4096,768]{1,0:T(8,128)(2,1)} slice(bf16[4096,1024]{1,0:T(8,128)(2,1)} %all-gather.2.cloned.1.call-done), slice={[0:4096], [256:1024]} | slice | bytes 12582912 | tf_op jit(solution)/shard_map/split | solution.py:55
  93.1 8.8 %copy.18 = bf16[4096,768]{0,1:T(8,128)(2,1)} copy(bf16[4096,768]{1,0:T(8,128)(2,1)} %split.9) | data formatting | bytes 12582912 | tf_op jit(solution)/shard_map/split | solution.py:55
  101.8 3.0 split.8
  104.9 4.1 %copy.17 = bf16[4096,256]{0,1:T(8,128)(2,1)} copy(bf16[4096,256]{1,0:T(8,128)(2,1)} %split.8) | data formatting | bytes 4194304 | tf_op jit(solution)/shard_map/split | solution.py:55
  109.0 4.1 %fusion = (f32[4,256]{1,0:T(4,128)S(1)}, f32[4,256,4096]{2,1,0:T(8,128)S(1)}) fusion(pred[4096]{0:T(1024)(128)(4,1)S(1)} %iota_compare_fusion, bf16[256,4,64]{0,2,1:T(8,128)(2,1)S(1)} %bitcast.49, bf16[4096,4,64]{0,2,1:T(8,128)(2,1)} %bitcast.47), kind=kOutput, calls=%fused_computation.2 | convolution fusion | flops 549452800 | bytes 19013632 | tf_op jit(solution)/shard_map/qhd,khd->hqk/dot_general | solution.py:64
  113.1 4.0 %fusion.1 = f32[4,256]{1,0:T(4,128)S(1)} fusion(f32[4,256,4096]{2,1,0:T(8,128)S(1)} %get-tuple-element.17, f32[4,256]{1,0:T(4,128)S(1)} %get-tuple-element.15, pred[4096]{0:T(1024)(128)(4,1)S(1)} %iota_compare_fusion), kind=kLoop, calls=%fused_computation.3 | loop fusion | flops 16776192 | bytes 16789504 | tf_op jit(solution)/shard_map/reduce_sum | solution.py:72
  117.2 1.7 copy-done.2
  118.8 10.3 %multiply_reduce_fusion = (f32[256]{0:T(256)S(1)}, f32[256,4,192]{0,2,1:T(8,128)S(1)}) fusion(f32[256,4]{0,1:T(4,128)S(1)} %bitcast.50, bf16[4096,4,192]{0,2,1:T(8,128)(2,1)} %bitcast.48, f32[4,256,4096]{2,1,0:T(8,128)} %copy-done.2, f32[4,256]{1,0:T(4,128)S(1)} %get-tuple-element.15, pred[4096]{0:T(1024)(128)(4,1)S(1)} %iota_compare_fusion, ...), kind=kOutput, calls=%fused_computation.68 | convolution fusion | flops 1628176128 | bytes 23872512 | tf_op jit(solution)/shard_map/hqk,khd->qhd/dot_general | solution.py:73
  130.0 2.7 broadcast_in_dim.33
  132.7 5.2 %convert_element_type.79 = f32[512,1536]{1,0:T(8,128)} reshape(f32[256,2,1536]{2,1,0:T(2,128)} %broadcast_in_dim.33) | data formatting | bytes 6291456 | tf_op jit(solution)/shard_map/convert_element_type | solution.py:90
  138.0 2.9 fusion.24
  140.9 3.1 collective-permute-start
  145.6 2.8 collective-permute-done.1
  148.4 6.6 %fusion.27 = f32[1536,1536]{1,0:T(8,128)} fusion(bf16[512,1536]{1,0:T(8,128)(2,1)S(1)} %fusion.24, bf16[1,1536]{1,0:T(2,128)(2,1)S(1)} %collective-permute-done.1, bf16[1,1536]{1,0:T(2,128)(2,1)S(1)} %collective-permute-done, bf16[1,512,1536]{2,1,0:T(8,128)(2,1)S(1)} %copy-done.5, f32[1536]{0:T(1024)S(1)} %get-tuple-element.7, ...), kind=kOutput, calls=%fused_computation.41 | convolution fusion | flops 2434007040 | bytes 12607488 | tf_op jit(solution)/shard_map/dot_general | solution.py:120
  155.0 7.5 %fusion.17 = bf16[512,1536]{1,0:T(8,128)(2,1)S(1)} fusion(bf16[1,1536]{1,0:T(2,128)(2,1)S(1)} %collective-permute-done.1, bf16[512,1536]{1,0:T(8,128)(2,1)S(1)} %fusion.24, bf16[1,1536]{1,0:T(2,128)(2,1)S(1)} %collective-permute-done, bf16[1536,1536]{1,0:T(8,128)(2,1)} %param.18, bf16[1,512,1536]{2,1,0:T(8,128)(2,1)} %param.19, ...), kind=kOutput, calls=%fused_computation.28 | convolution fusion | flops 2442657792 | bytes 9461760 | tf_op jit(solution)/shard_map/dot_general | solution.py:101
  163.9 4.0 %collective-permute-start.3 = (bf16[1,1536]{1,0:T(2,128)(2,1)S(1)}, bf16[1,1536]{1,0:T(2,128)(2,1)S(1)}, u32[]{:S(2)}, u32[]{:S(2)}) collective-permute-start(bf16[1,1536]{1,0:T(2,128)(2,1)S(1)} %get-tuple-element.11), channel_id=1, source_target_pairs={{0,1},{1,2},{2,3},{3,4},{4,5},{5,6},{6,7},{7,8},{8,9},{9,10},{10,1... | collective-permute-start | bytes 9224 | tf_op jit(solution)/shard_map/ppermute | solution.py:21
  168.7 3.5 %fusion.18 = (f32[1536]{0:T(1024)S(1)}, f32[1536]{0:T(1024)S(1)}, f32[1536]{0:T(1024)S(1)}, bf16[1,512,1536]{2,1,0:T(8,128)(2,1)}) fusion(bf16[512,1536]{1,0:T(8,128)(2,1)S(1)} %fusion.17, bf16[512,1536]{1,0:T(8,128)(2,1)S(1)} %fusion.24, bf16[1,1536]{1,0:T(2,128)(2,1)S(1)} %collective-permute-done, bf16[1,1536]{1,0:T(2,128)(2,1)S(1)} %collective-permute-done.1, ...), kind=kLoop, calls=%fused_computation.29 | loop fusion | flops 23588352 | bytes 4767744 | tf_op jit(solution)/shard_map/reduce_sum | solution.py:109
  172.2 74.9 %psum.15 = f32[3,1536]{1,0:T(4,128)S(1)} all-reduce(f32[3,1536]{1,0:T(4,128)S(1)} %pad_maximum_fusion.6), channel_id=1, replica_groups=mesh['dp'=8,'seq'=16] {'dp','seq'}, use_global_device_ids=true, to_apply=%region_7.8 | all-reduce | flops 4608 | bytes 36864 | tf_op jit(solution)/shard_map/psum | solution.py:123
  247.7 75.5 %all-reduce.2.cloned.1.call-done = f32[1536,1536]{1,0:T(8,128)} async-done(((f32[1536,1536]{1,0:T(8,128)}), f32[1536,1536]{1,0:T(8,128)}) %all-reduce.2.cloned.1.call-update) | async-done | bytes 9437200 | tf_op jit(solution)/shard_map/psum | solution.py:123
  323.3 7.2 %multiply_convert_fusion = bf16[1536,1536]{1,0:T(8,128)(2,1)} fusion(f32[1536,1536]{1,0:T(8,128)} %all-reduce.2.cloned.1.call-done), kind=kLoop, calls=%fused_computation.5 | loop fusion | flops 4718592 | bytes 14155776 | tf_op jit(solution)/shard_map/convert_element_type | solution.py:124
  (35 shorter events, 6.2 us)
Async XLA Ops:
  7.2 122.0 %copy-start = (bf16[768,1536]{1,0:T(8,128)(2,1)S(1)}, bf16[768,1536]{1,0:T(8,128)(2,1)}, u32[]{:S(2)}) copy-start(bf16[768,1536]{1,0:T(8,128)(2,1)} %param.16) | copy-start | bytes 7077892
  7.2 80.0 %all-gather.2.cloned.1.call-start = ((), (), s32[]{:S(2)}) async-start(), calls=%async_computation | async-start | bytes 8912896 | tf_op jit(solution)/shard_map/all_gather | solution.py:56
  9.2 4.5 %copy-start.3 = (bf16[1,256,1536]{2,1,0:T(8,128)(2,1)S(1)}, bf16[1,256,1536]{2,1,0:T(8,128)(2,1)}, u32[]{:S(2)}) copy-start(bf16[1,256,1536]{2,1,0:T(8,128)(2,1)} %param.10) | copy-start | bytes 2359300
  12.9 310.3 %all-reduce.2.cloned.1.call-start = ((), (), s32[]{:S(2)}) async-start(), calls=%async_computation.1 | async-start | bytes 18874368 | tf_op jit(solution)/shard_map/psum | solution.py:123
  113.1 5.7 %copy-start.2 = (f32[4,256,4096]{2,1,0:T(8,128)}, f32[4,256,4096]{2,1,0:T(8,128)S(1)}, u32[]{:S(2)}) copy-start(f32[4,256,4096]{2,1,0:T(8,128)S(1)} %get-tuple-element.17) | copy-start | bytes 50331652
  138.0 7.6 %copy-start.4 = (f32[3,1536]{1,0:T(4,128)S(1)}, f32[3,1536]{1,0:T(4,128)}, u32[]{:S(2)}) copy-start(f32[3,1536]{1,0:T(4,128)} %param.17) | copy-start | bytes 55300
  138.0 10.4 %copy-start.5 = (bf16[1,512,1536]{2,1,0:T(8,128)(2,1)S(1)}, bf16[1,512,1536]{2,1,0:T(8,128)(2,1)}, u32[]{:S(2)}) copy-start(bf16[1,512,1536]{2,1,0:T(8,128)(2,1)} %param.19) | copy-start | bytes 4718596
  140.9 4.7 %collective-permute-start = (bf16[1,1536]{1,0:T(2,128)(2,1)S(1)}, bf16[1,1536]{1,0:T(2,128)(2,1)S(1)}, u32[]{:S(2)}, u32[]{:S(2)}) collective-permute-start(bf16[1,1536]{1,0:T(2,128)(2,1)S(1)} %get-tuple-element.12), channel_id=1, source_target_pairs={{0,1},{1,2},{2,3},{3,4},{4,5},{5,6},{6,7},{7,8},{8,9},{9,10},{10,1... | collective-permute-start | bytes 9224 | tf_op jit(solution)/shard_map/ppermute | solution.py:21
  144.1 4.4 %collective-permute-start.1 = (bf16[1,1536]{1,0:T(2,128)(2,1)S(1)}, bf16[1,1536]{1,0:T(2,128)(2,1)S(1)}, u32[]{:S(2)}, u32[]{:S(2)}) collective-permute-start(bf16[1,1536]{1,0:T(2,128)(2,1)S(1)} %get-tuple-element.13), channel_id=1, source_target_pairs={{1,0},{2,1},{3,2},{4,3},{5,4},{6,5},{7,6},{8,7},{9,8},{10,9},{11,1... | collective-permute-start | bytes 9224 | tf_op jit(solution)/shard_map/ppermute | solution.py:23
  162.6 5.3 %collective-permute-start.2 = (bf16[1,1536]{1,0:T(2,128)(2,1)S(1)}, bf16[1,1536]{1,0:T(2,128)(2,1)S(1)}, u32[]{:S(2)}, u32[]{:S(2)}) collective-permute-start(bf16[1,1536]{1,0:T(2,128)(2,1)S(1)} %get-tuple-element.10), channel_id=1, source_target_pairs={{1,0},{2,1},{3,2},{4,3},{5,4},{6,5},{7,6},{8,7},{9,8},{10,9},{11,1... | collective-permute-start | bytes 9224 | tf_op jit(solution)/shard_map/ppermute | solution.py:23
  163.9 4.8 %collective-permute-start.3 = (bf16[1,1536]{1,0:T(2,128)(2,1)S(1)}, bf16[1,1536]{1,0:T(2,128)(2,1)S(1)}, u32[]{:S(2)}, u32[]{:S(2)}) collective-permute-start(bf16[1,1536]{1,0:T(2,128)(2,1)S(1)} %get-tuple-element.11), channel_id=1, source_target_pairs={{0,1},{1,2},{2,3},{3,4},{4,5},{5,6},{6,7},{7,8},{8,9},{9,10},{10,1... | collective-permute-start | bytes 9224 | tf_op jit(solution)/shard_map/ppermute | solution.py:21
  323.3 7.2 %copy-start.1 = (bf16[768,1536]{1,0:T(8,128)(2,1)S(1)}, bf16[768,1536]{1,0:T(8,128)(2,1)}, u32[]{:S(2)}) copy-start(bf16[768,1536]{1,0:T(8,128)(2,1)} %param.16) | copy-start | bytes 7077892
Sparse Core Ops, SparseCore 0:
  13.0 74.0 all-gather.1
  155.2 168.0 all-reduce.1
